TPU v7x, 32 devices: a whole 2x2x4 slice. The times are simulated.
32 devices in a mesh: seq: 4 (over x, core), rows: 8 (over z, y).
Axes of the slice: x: 2, y: 2, z: 4, core: 2. Of those that a mesh axis runs over, the one named last changes fastest.
Arguments:
- patches: bfloat16 [16, 1024, 768], P('rows', 'seq'), may hold values from -6 to 6
- segments: int32 [16, 1024], P('rows', 'seq'), may hold values from 0 to 8, as said below
- masked: int32 [16, 1024], P('rows', 'seq'), may hold values 0 or 1
- mask_embedding: bfloat16 [768], P(('seq', 'rows')), may hold values from -5 to 5
- norm1_gain: bfloat16 [768], P(('seq', 'rows')), may hold values from 0.5 to 1.5
- norm1_bias: bfloat16 [768], P(('seq', 'rows')), may hold values from -4 to 4
- qkv_weight: bfloat16 [768, 2304], P(('seq', 'rows')), may hold values from -0.21875 to 0.21875
- query_bias: bfloat16 [768], P(('seq', 'rows')), may hold values from -4 to 4
- value_bias: bfloat16 [768], P(('seq', 'rows')), may hold values from -0.75 to 0.75
- out_weight: bfloat16 [768, 768], P(('seq', 'rows')), may hold values from -3.5 to 3.5
- out_bias: bfloat16 [768], P(('seq', 'rows')), may hold values from -4 to 4
- norm2_gain: bfloat16 [768], P(('seq', 'rows')), may hold values from 0.5 to 1.5
- norm2_bias: bfloat16 [768], P(('seq', 'rows')), may hold values from -4 to 4
- up_weight: bfloat16 [768, 3072], P(('seq', 'rows')), may hold values from -0.21875 to 0.21875
- up_bias: bfloat16 [3072], P(('seq', 'rows')), may hold values from -4 to 4
- down_weight: bfloat16 [3072, 768], P(('seq', 'rows')), may hold values from -0.109375 to 0.109375
- down_bias: bfloat16 [768], P(('seq', 'rows')), may hold values from -4 to 4
- cotangent: bfloat16 [16, 1024, 768], P('rows', 'seq'), may hold values from -6 to 6
Outputs:
- output: bfloat16 [16, 1024, 768], P('rows', 'seq')
- input_grad: float32 [16, 1024, 768], P('rows', 'seq')
- mask_embedding_grad: float32 [768], P(('seq', 'rows'))
- norm1_gain_grad: float32 [768], P(('seq', 'rows'))
- norm1_bias_grad: float32 [768], P(('seq', 'rows'))
- qkv_weight_grad: float32 [768, 2304], P(('seq', 'rows'))
- query_bias_grad: float32 [768], P(('seq', 'rows'))
- value_bias_grad: float32 [768], P(('seq', 'rows'))
- out_weight_grad: float32 [768, 768], P(('seq', 'rows'))
- out_bias_grad: float32 [768], P(('seq', 'rows'))
- norm2_gain_grad: float32 [768], P(('seq', 'rows'))
- norm2_bias_grad: float32 [768], P(('seq', 'rows'))
- up_weight_grad: float32 [768, 3072], P(('seq', 'rows'))
- up_bias_grad: float32 [3072], P(('seq', 'rows'))
- down_weight_grad: float32 [3072, 768], P(('seq', 'rows'))
- down_bias_grad: float32 [768], P(('seq', 'rows'))
Inputs may be any that keep to these rules, and one draw needn't show every extreme that they name: `segments`: along each row the ids never fall except to 0; 0 (padding) stands only in the last fewer than 64 positions of a row; in the first of every 2 rows one clip covers patches of every index of seq.
All inputs are finite; a program needn't handle non-finite values. No bound on the sum of `masked` on one device may be relied on, other than what follows from the above.
Results may differ from a plain program's by a relative error of at most 0.017.
Values may be sent and summed in bfloat16 or wider, within the bound.
No kernel may reach another device: no remote copies, remote signals or barrier semaphores. Data moves between devices by JAX's collectives and lax.ppermute only.
A program may use at most 192 MiB of HBM per device.

v0:
```python
import jax
import jax.numpy as jnp
from jax import lax
from jax.sharding import PartitionSpec as P

HEADS = 12
HEAD_SIZE = 64


EPSILON = 1e-06
FLOOR_SCORE = -1e30
HALF_ROOT = 0.7071067811865476


def layer_norm(inputs, gain, shift):
    mean = jnp.mean(inputs, axis=-1, keepdims=True)
    centered = inputs - mean
    spread = jnp.mean(centered * centered, axis=-1, keepdims=True)
    return centered * lax.rsqrt(spread + EPSILON) * gain + shift


def gelu_exact(inputs):
    return 0.5 * inputs * (1.0 + lax.erf(inputs * HALF_ROOT))


def contract_rows(left, right):
    return lax.dot_general(
        left, right, (((0,), (0,)), ((), ())), preferred_element_type=jnp.float32
    )


def contract_cols(left, right):
    return lax.dot_general(
        left, right, (((1,), (1,)), ((), ())), preferred_element_type=jnp.float32
    )


def block_scores(queries, query_segment, key_block, key_segment):
    row_count, count = (key_block.shape[0], key_block.shape[1])
    key_heads = key_block.reshape(row_count, count, HEADS, HEAD_SIZE)
    scores = jnp.einsum("rqhe,rkhe->rhqk", queries, key_heads, preferred_element_type=jnp.float32)
    allowed = (query_segment[:, None, :, None] == key_segment[:, None, None, :]) & (
        key_segment[:, None, None, :] > 0
    )
    return (jnp.where(allowed, scores, FLOOR_SCORE), allowed, key_heads)


def fold_forward(queries, query_segment, carry, pieces):
    running, total, summed = carry
    key_block, value_block, key_segment = pieces
    row_count, count = (key_block.shape[0], key_block.shape[1])
    scores, allowed, key_heads = block_scores(queries, query_segment, key_block, key_segment)
    highest = jnp.maximum(running, jnp.max(scores, axis=-1))
    weights = jnp.where(allowed, jnp.exp(scores - highest[..., None]), 0.0)
    total = jnp.sum(weights, axis=-1)
    value_heads = value_block.reshape(row_count, count, HEADS, HEAD_SIZE)
    update = jnp.einsum(
        "rhqk,rkhe->rqhe",
        weights.astype(jnp.bfloat16),
        value_heads,
        preferred_element_type=jnp.float32,
    )
    summed = update
    return (highest, total, summed)


def block_grads(
    queries, query_segment, d_mixed, log_total, delta, key_block, value_block, key_segment
):
    row_count, count = (key_block.shape[0], key_block.shape[1])
    scores, allowed, key_heads = block_scores(queries, query_segment, key_block, key_segment)
    probs = jnp.where(allowed, jnp.exp(scores - log_total[..., None]), 0.0)
    value_heads = value_block.reshape(row_count, count, HEADS, HEAD_SIZE)
    d_probs = jnp.einsum(
        "rqhe,rkhe->rhqk", d_mixed, value_heads, preferred_element_type=jnp.float32
    )
    d_scores = (probs * (d_probs - delta[..., None])).astype(jnp.bfloat16)
    d_query = jnp.einsum("rhqk,rkhe->rqhe", d_scores, key_heads, preferred_element_type=jnp.float32)
    d_key = jnp.einsum("rhqk,rqhe->rkhe", d_scores, queries, preferred_element_type=jnp.float32)
    d_value = jnp.einsum(
        "rhqk,rqhe->rkhe", probs.astype(jnp.bfloat16), d_mixed, preferred_element_type=jnp.float32
    )
    width = HEADS * HEAD_SIZE
    return (
        d_query,
        d_key.reshape(row_count, count, width),
        d_value.reshape(row_count, count, width),
    )


def fold_back(queries, query_segment, d_mixed, log_total, delta, pieces):
    key_block, value_block, key_segment = pieces
    part_query, part_key, part_value = block_grads(
        queries, query_segment, d_mixed, log_total, delta, key_block, value_block, key_segment
    )
    return (part_query, part_key, part_value)


def body(
    patches,
    segments,
    masked,
    mask_embedding,
    norm1_gain,
    norm1_bias,
    qkv_weight,
    query_bias,
    value_bias,
    out_weight,
    out_bias,
    norm2_gain,
    norm2_bias,
    up_weight,
    up_bias,
    down_weight,
    down_bias,
    cotangent,
):
    gathered = (
        lax.all_gather(mask_embedding, ("seq", "rows"), axis=0, tiled=True),
        lax.all_gather(norm1_gain, ("seq", "rows"), axis=0, tiled=True),
        lax.all_gather(norm1_bias, ("seq", "rows"), axis=0, tiled=True),
        lax.all_gather(qkv_weight, ("seq", "rows"), axis=0, tiled=True),
        lax.all_gather(query_bias, ("seq", "rows"), axis=0, tiled=True),
        lax.all_gather(value_bias, ("seq", "rows"), axis=0, tiled=True),
        lax.all_gather(out_weight, ("seq", "rows"), axis=0, tiled=True),
        lax.all_gather(out_bias, ("seq", "rows"), axis=0, tiled=True),
        lax.all_gather(norm2_gain, ("seq", "rows"), axis=0, tiled=True),
        lax.all_gather(norm2_bias, ("seq", "rows"), axis=0, tiled=True),
        lax.all_gather(up_weight, ("seq", "rows"), axis=0, tiled=True),
        lax.all_gather(up_bias, ("seq", "rows"), axis=0, tiled=True),
        lax.all_gather(down_weight, ("seq", "rows"), axis=0, tiled=True),
        lax.all_gather(down_bias, ("seq", "rows"), axis=0, tiled=True),
    )
    (
        embed,
        gain_one,
        shift_one,
        w_project,
        bias_query,
        bias_value,
        w_out,
        bias_out,
        gain_two,
        shift_two,
        w_up,
        bias_up,
        w_down,
        bias_down,
    ) = gathered
    embed = embed.astype(jnp.float32)
    gain_one = gain_one.astype(jnp.float32)
    shift_one = shift_one.astype(jnp.float32)
    bias_query = bias_query.astype(jnp.float32)
    bias_value = bias_value.astype(jnp.float32)
    bias_out = bias_out.astype(jnp.float32)
    gain_two = gain_two.astype(jnp.float32)
    shift_two = shift_two.astype(jnp.float32)
    bias_up = bias_up.astype(jnp.float32)
    bias_down = bias_down.astype(jnp.float32)
    row_count, patch_count, width = patches.shape
    tokens = row_count * patch_count
    scale = HEAD_SIZE ** (-0.5)
    heads_shape = (row_count, patch_count, HEADS, HEAD_SIZE)
    is_masked = masked.reshape(tokens) == 1
    embedded = jnp.where(
        is_masked[:, None], embed[None, :], patches.reshape(tokens, width).astype(jnp.float32)
    )
    normed_full, pull_one = jax.vjp(layer_norm, embedded, gain_one, shift_one)
    normed_one = normed_full.astype(jnp.bfloat16)
    projected = jnp.dot(normed_one, w_project, preferred_element_type=jnp.float32)
    queries = (
        ((projected[:, :width] + bias_query) * scale).astype(jnp.bfloat16).reshape(heads_shape)
    )
    key_rows = (
        projected[:, width : 2 * width].astype(jnp.bfloat16).reshape(row_count, patch_count, width)
    )
    value_rows = (
        (projected[:, 2 * width :] + bias_value)
        .astype(jnp.bfloat16)
        .reshape(row_count, patch_count, width)
    )
    segment_ids = segments.astype(jnp.bfloat16)
    initial = (
        jnp.full((row_count, HEADS, patch_count), FLOOR_SCORE, jnp.float32),
        jnp.zeros((row_count, HEADS, patch_count), jnp.float32),
        jnp.zeros(heads_shape, jnp.float32),
    )
    running, total, summed = fold_forward(
        queries,
        segment_ids,
        initial,
        (
            lax.all_gather(key_rows, "seq", axis=1, tiled=True),
            lax.all_gather(value_rows, "seq", axis=1, tiled=True),
            lax.all_gather(segment_ids, "seq", axis=1, tiled=True),
        ),
    )
    safe_total = jnp.where(total > 0, total, 1.0)
    mixed_heads = summed / jnp.transpose(safe_total, (0, 2, 1))[..., None]
    log_total = running + jnp.log(safe_total)
    mixed = mixed_heads.reshape(tokens, width).astype(jnp.bfloat16)
    middle = embedded + jnp.dot(mixed, w_out, preferred_element_type=jnp.float32) + bias_out
    normed_mid, pull_two = jax.vjp(layer_norm, middle, gain_two, shift_two)
    normed_two = normed_mid.astype(jnp.bfloat16)
    hidden = jnp.dot(normed_two, w_up, preferred_element_type=jnp.float32) + bias_up
    activated_full, pull_act = jax.vjp(gelu_exact, hidden)
    activated = activated_full.astype(jnp.bfloat16)
    result = middle + jnp.dot(activated, w_down, preferred_element_type=jnp.float32) + bias_down
    output = result.astype(jnp.bfloat16).reshape(row_count, patch_count, width)
    d_result = cotangent.reshape(tokens, width).astype(jnp.float32)
    d_branch = d_result.astype(jnp.bfloat16)
    grad_down = contract_rows(activated, d_branch)
    grad_down_bias = jnp.sum(d_branch.astype(jnp.float32), axis=0)
    (d_hidden_full,) = pull_act(contract_cols(d_branch, w_down))
    d_hidden = d_hidden_full.astype(jnp.bfloat16)
    grad_up = contract_rows(normed_two, d_hidden)
    grad_up_bias = jnp.sum(d_hidden.astype(jnp.float32), axis=0)
    d_norm_mid, grad_gain_two, grad_shift_two = pull_two(contract_cols(d_hidden, w_up))
    d_middle = d_result + d_norm_mid
    d_attn = d_middle.astype(jnp.bfloat16)
    grad_out = contract_rows(mixed, d_attn)
    grad_out_bias = jnp.sum(d_attn.astype(jnp.float32), axis=0)
    d_mixed = contract_cols(d_attn, w_out).astype(jnp.bfloat16).reshape(heads_shape)
    delta = jnp.transpose(jnp.sum(d_mixed.astype(jnp.float32) * mixed_heads, axis=-1), (0, 2, 1))
    d_query, key_grad, value_grad = fold_back(
        queries,
        segment_ids,
        d_mixed,
        log_total,
        delta,
        (
            lax.all_gather(key_rows, "seq", axis=1, tiled=True),
            lax.all_gather(value_rows, "seq", axis=1, tiled=True),
            lax.all_gather(segment_ids, "seq", axis=1, tiled=True),
        ),
    )
    d_key, d_value = (
        lax.psum_scatter(
            key_grad.astype(jnp.bfloat16), "seq", scatter_dimension=1, tiled=True
        ).astype(jnp.float32),
        lax.psum_scatter(
            value_grad.astype(jnp.bfloat16), "seq", scatter_dimension=1, tiled=True
        ).astype(jnp.float32),
    )
    query_low = d_query.reshape(tokens, width).astype(jnp.bfloat16)
    key_low = d_key.reshape(tokens, width).astype(jnp.bfloat16)
    value_low = d_value.reshape(tokens, width).astype(jnp.bfloat16)
    d_projected = jnp.concatenate([query_low * jnp.bfloat16(scale), key_low, value_low], axis=1)
    grad_project = contract_rows(normed_one, d_projected)
    grad_query_bias = jnp.sum(query_low.astype(jnp.float32), axis=0) * scale
    grad_value_bias = jnp.sum(value_low.astype(jnp.float32), axis=0)
    d_norm_in, grad_gain_one, grad_shift_one = pull_one(contract_cols(d_projected, w_project))
    d_embedded = d_middle + d_norm_in
    input_grad = jnp.where(is_masked[:, None], 0.0, d_embedded).reshape(
        row_count, patch_count, width
    )
    grad_embed = jnp.sum(jnp.where(is_masked[:, None], d_embedded, 0.0), axis=0)
    summed_grads = (
        lax.psum_scatter(grad_embed, ("seq", "rows"), scatter_dimension=0, tiled=True),
        lax.psum_scatter(grad_gain_one, ("seq", "rows"), scatter_dimension=0, tiled=True),
        lax.psum_scatter(grad_shift_one, ("seq", "rows"), scatter_dimension=0, tiled=True),
        lax.psum_scatter(grad_project, ("seq", "rows"), scatter_dimension=0, tiled=True),
        lax.psum_scatter(grad_query_bias, ("seq", "rows"), scatter_dimension=0, tiled=True),
        lax.psum_scatter(grad_value_bias, ("seq", "rows"), scatter_dimension=0, tiled=True),
        lax.psum_scatter(grad_out, ("seq", "rows"), scatter_dimension=0, tiled=True),
        lax.psum_scatter(grad_out_bias, ("seq", "rows"), scatter_dimension=0, tiled=True),
        lax.psum_scatter(grad_gain_two, ("seq", "rows"), scatter_dimension=0, tiled=True),
        lax.psum_scatter(grad_shift_two, ("seq", "rows"), scatter_dimension=0, tiled=True),
        lax.psum_scatter(grad_up, ("seq", "rows"), scatter_dimension=0, tiled=True),
        lax.psum_scatter(grad_up_bias, ("seq", "rows"), scatter_dimension=0, tiled=True),
        lax.psum_scatter(grad_down, ("seq", "rows"), scatter_dimension=0, tiled=True),
        lax.psum_scatter(grad_down_bias, ("seq", "rows"), scatter_dimension=0, tiled=True),
    )
    return (
        output,
        input_grad,
        summed_grads[0],
        summed_grads[1],
        summed_grads[2],
        summed_grads[3],
        summed_grads[4],
        summed_grads[5],
        summed_grads[6],
        summed_grads[7],
        summed_grads[8],
        summed_grads[9],
        summed_grads[10],
        summed_grads[11],
        summed_grads[12],
        summed_grads[13],
    )


def solution(mesh):
    placed = (
        P("rows", "seq", None),
        P("rows", "seq"),
        P("rows", "seq"),
        P(("seq", "rows")),
        P(("seq", "rows")),
        P(("seq", "rows")),
        P(("seq", "rows"), None),
        P(("seq", "rows")),
        P(("seq", "rows")),
        P(("seq", "rows"), None),
        P(("seq", "rows")),
        P(("seq", "rows")),
        P(("seq", "rows")),
        P(("seq", "rows"), None),
        P(("seq", "rows")),
        P(("seq", "rows"), None),
        P(("seq", "rows")),
        P("rows", "seq", None),
    )
    return jax.shard_map(
        body,
        mesh=mesh,
        in_specs=placed,
        out_specs=(
            P("rows", "seq", None),
            P("rows", "seq", None),
            P(("seq", "rows")),
            P(("seq", "rows")),
            P(("seq", "rows")),
            P(("seq", "rows"), None),
            P(("seq", "rows")),
            P(("seq", "rows")),
            P(("seq", "rows"), None),
            P(("seq", "rows")),
            P(("seq", "rows")),
            P(("seq", "rows")),
            P(("seq", "rows"), None),
            P(("seq", "rows")),
            P(("seq", "rows"), None),
            P(("seq", "rows")),
        ),
        check_vma=False,
    )
```

profile of v0, /device:TPU:0, one launch (start us, length us, event | category | flops | bytes accessed | tf_op | source)
XLA Modules:
  0.0 981.2 jit_solution(7794681425478045320)
XLA Ops:
  17.1 42.5 %all-reduce.21 = (bf16[768]{0:T(1024)(128)(2,1)S(1)}, bf16[768]{0:T(1024)(128)(2,1)S(1)}, bf16[768]{0:T(1024)(128)(2,1)S(1)}, bf16[768]{0:T(1024)(128)(2,1)S(1)}...) all-reduce(bf16[768]{0:T(1024)(128)(2,1)S(1)} %dynamic-update-slice, ...), channel_id=1, replica_groups=mesh['seq'=4,'rows'=8] {'seq','rows'}, use_global_device_ids=true, to_apply=%add | all-reduce | flops 9984 | bytes 39936
  64.5 9.3 all-gather.7.cloned.1.call-done
  93.6 15.0 %all-gather.11.cloned.1.call-done = bf16[2,1024,768]{2,1,0:T(8,128)(2,1)} async-done(((bf16[2,256,768]{2,1,0:T(8,128)(2,1)}), bf16[2,1024,768]{2,1,0:T(8,128)(2,1)}) %all-gather.11.cloned.1.call-update) | async-done | bytes 3145744 | tf_op jit(solution)/shard_map/all_gather | solution.py:194
  112.0 26.7 %all-gather.9.cloned.1.call-done = bf16[2,1024,768]{2,1,0:T(8,128)(2,1)} async-done(((bf16[2,256,768]{2,1,0:T(8,128)(2,1)}), bf16[2,1024,768]{2,1,0:T(8,128)(2,1)}) %all-gather.9.cloned.1.call-update) | async-done | bytes 3145744 | tf_op jit(solution)/shard_map/all_gather | solution.py:195
  143.4 11.8 %select_reduce_fusion = (f32[2,12,256]{2,1,0:T(8,128)S(1)}, f32[2,12,256,1024]{3,2,1,0:T(8,128)}) fusion(pred[2,256,1024]{2,1,0:T(8,128)(4,1)} %compare_and_fusion, bf16[2,1024,12,64]{1,3,2,0:T(8,128)(2,1)S(1)} %bitcast.90, bf16[2,256,12,64]{1,0,3,2:T(2,128)(2,1)} %reshape.225), kind=kOutput, calls=%fused_computation.3 | convolution fusion | flops 817883136 | bytes 29646848 | tf_op jit(solution)/shard_map/rqhe,rkhe->rhqk/dot_general | solution.py:41
  155.1 12.4 %fusion = f32[2,12,256]{2,1,0:T(8,128)S(1)} fusion(f32[2,12,256,1024]{3,2,1,0:T(8,128)} %get-tuple-element.60, f32[2,12,256]{2,1,0:T(8,128)S(1)} %broadcast_maximum_fusion, pred[2,256,1024]{2,1,0:T(8,128)(4,1)S(1)} %copy-done.9), kind=kLoop, calls=%fused_computation.4 | loop fusion | flops 25159680 | bytes 25739264 | tf_op jit(solution)/shard_map/reduce_sum | solution.py:55
  167.6 13.0 %fusion.43 = (bf16[2,256,12,64]{1,3,2,0:T(8,128)(2,1)S(1)}, f32[2,256,12,64]{1,3,2,0:T(8,128)}) fusion(f32[2,256,12]{1,2,0:T(8,128)S(1)} %compare_select_fusion.1, bf16[2,1024,12,64]{1,3,2,0:T(8,128)(2,1)} %bitcast.96, f32[2,12,256,1024]{3,2,1,0:T(8,128)} %get-tuple-element.60, f32[2,12,256]{2,1,0:T(8,128)S(1)} %broadcast_maximum_fusion, ...), kind=kOutput, calls=%fused_computation.91 | convolution fusion | flops 831258624 | bytes 31244288 | tf_op jit(solution)/shard_map/rhqk,rkhe->rqhe/dot_general | solution.py:57
  182.4 13.3 %all-gather.13.cloned.1.call-done = bf16[768,768]{1,0:T(8,128)(2,1)} async-done(((bf16[24,768]{1,0:T(8,128)(2,1)}), bf16[768,768]{1,0:T(8,128)(2,1)}) %all-gather.13.cloned.1.call-update) | async-done | bytes 1179664 | tf_op jit(solution)/shard_map/all_gather | solution.py:126
  200.1 61.0 %all-gather.15.cloned.1.call-done = bf16[768,3072]{1,0:T(8,128)(2,1)} async-done(((bf16[24,3072]{1,0:T(8,128)(2,1)}), bf16[768,3072]{1,0:T(8,128)(2,1)}) %all-gather.15.cloned.1.call-update) | async-done | bytes 4718608 | tf_op jit(solution)/shard_map/all_gather | solution.py:130
  261.1 8.2 fusion.39
  269.3 57.0 %all-gather.17.cloned.1.call-done = bf16[3072,768]{1,0:T(8,128)(2,1)} async-done(((bf16[96,768]{1,0:T(8,128)(2,1)}), bf16[3072,768]{1,0:T(8,128)(2,1)}) %all-gather.17.cloned.1.call-update) | async-done | bytes 4718608 | tf_op jit(solution)/shard_map/all_gather | solution.py:132
  326.3 10.0 %convert_reduce_fusion = (f32[3072]{0:T(1024)S(1)}, bf16[512,3072]{1,0:T(8,128)(2,1)S(1)}, bf16[512,3072]{1,0:T(8,128)(2,1)}) fusion(f32[512,3072]{1,0:T(8,128)} %fusion.39, f32[3072]{0:T(1024)S(1)} %convert_element_type.167, bf16[512,768]{1,0:T(8,128)(2,1)} %bitcast.93, bf16[3072,768]{1,0:T(8,128)(2,1)} %all-gather.17.cloned.1.call-done), kind=kOutput, calls=%fused_computation.11 | convolution fusion | flops 2444227584 | bytes 18112512 | tf_op jit(solution)/shard_map/dot_general | solution.py:33
  351.2 18.1 %multiply_convert_fusion = bf16[2,12,256,1024]{3,2,1,0:T(8,128)(2,1)} fusion(f32[2,12,256,1024]{3,2,1,0:T(8,128)} %get-tuple-element.60, f32[2,12,256]{2,1,0:T(8,128)S(1)} %bitcast.109, f32[2,12,256]{2,1,0:T(8,128)S(1)} %fusion.29, pred[2,256,1024]{2,1,0:T(8,128)(4,1)} %compare_and_fusion, bf16[2,1024,12,64]{1,3,2,0:T(8,128)(2,1)} %bitcast.97, ...), kind=kOutput, calls=%fused_computation | convolution fusion | flops 843055104 | bytes 42254336 | tf_op jit(solution)/shard_map/rqhe,rkhe->rhqk/dot_general | solution.py:74
  369.3 8.8 convolution_convert_fusion
  382.8 14.9 %fusion.9 = bf16[2,12,64,1024]{3,2,1,0:T(8,128)(2,1)} fusion(f32[2,12,256,1024]{3,2,1,0:T(8,128)} %get-tuple-element.60, f32[2,12,256]{2,1,0:T(8,128)S(1)} %fusion.29, pred[2,256,1024]{2,1,0:T(8,128)(4,1)} %compare_and_fusion, bf16[2,256,12,64]{1,0,3,2:T(2,128)(2,1)} %reshape.230), kind=kOutput, calls=%fused_computation.18 | convolution fusion | flops 832045056 | bytes 29646848 | tf_op jit(solution)/shard_map/rhqk,rqhe->rkhe/dot_general | solution.py:80
  406.0 8.9 fusion.38
  415.1 8.4 fusion.47
  423.8 9.1 convert_reduce_fusion.4
  435.4 24.9 %reduce-scatter.9.cloned.1.call-done = bf16[2,256,768]{2,1,0:T(8,128)(2,1)} async-done(((bf16[2,1024,768]{2,1,0:T(8,128)(2,1)}), bf16[2,256,768]{2,1,0:T(8,128)(2,1)}) %reduce-scatter.9.cloned.1.call-update) | async-done | bytes 786448 | tf_op jit(solution)/shard_map/reduce_scatter | solution.py:242
  481.2 40.3 %all-reduce.20 = (f32[768]{0:T(1024)S(1)}, f32[768]{0:T(1024)S(1)}, f32[768]{0:T(1024)S(1)}, f32[768]{0:T(1024)S(1)}, f32[768]{0:T(1024)S(1)}, /*index=5*/f32[76...) all-reduce(f32[768]{0:T(1024)S(1)} %get-tuple-element.53, ...), channel_id=4, replica_groups=mesh['seq'=4,'rows'=8] {'seq','rows'}, use_global_device_ids=true, to_apply=%region_14.15.clone | all-reduce | flops 9984 | bytes 79872
  527.3 38.4 %reduce-scatter.13.cloned.1.call-done = f32[24,768]{1,0:T(8,128)} async-done(((f32[768,768]{1,0:T(8,128)}), f32[24,768]{1,0:T(8,128)}) %reduce-scatter.13.cloned.1.call-update) | async-done | bytes 73744 | tf_op jit(solution)/shard_map/reduce_scatter | solution.py:266
  565.7 141.8 %reduce-scatter.15.cloned.1.call-done = f32[24,3072]{1,0:T(8,128)} async-done(((f32[768,3072]{1,0:T(8,128)}), f32[24,3072]{1,0:T(8,128)}) %reduce-scatter.15.cloned.1.call-update) | async-done | bytes 294928 | tf_op jit(solution)/shard_map/reduce_scatter | solution.py:270
  707.6 141.1 %reduce-scatter.17.cloned.1.call-done = f32[96,768]{1,0:T(8,128)} async-done(((f32[3072,768]{1,0:T(8,128)}), f32[96,768]{1,0:T(8,128)}) %reduce-scatter.17.cloned.1.call-update) | async-done | bytes 294928 | tf_op jit(solution)/shard_map/reduce_scatter | solution.py:272
  848.7 125.3 %reduce-scatter.11.cloned.1.call-done = f32[24,2304]{1,0:T(8,128)} async-done(((f32[768,2304]{1,0:T(8,128)}), f32[24,2304]{1,0:T(8,128)}) %reduce-scatter.11.cloned.1.call-update) | async-done | bytes 221200 | tf_op jit(solution)/shard_map/reduce_scatter | solution.py:263
  (171 shorter events, 105.8 us)
Async XLA Ops:
  7.2 55.5 %copy-start.2 = (bf16[2,256,768]{2,1,0:T(8,128)(2,1)S(1)}, bf16[2,256,768]{2,1,0:T(8,128)(2,1)}, u32[]{:S(2)}) copy-start(bf16[2,256,768]{2,1,0:T(8,128)(2,1)} %param.18) | copy-start | bytes 2359300
  7.2 66.6 %all-gather.7.cloned.1.call-start = ((), (), s32[]{:S(2)}) async-start(), calls=%async_computation.6 | async-start | bytes 3649536 | tf_op jit(solution)/shard_map/all_gather | solution.py:123
  7.9 100.7 %all-gather.11.cloned.1.call-start = ((), (), s32[]{:S(2)}) async-start(), calls=%async_computation.8 | async-start | bytes 3932160 | tf_op jit(solution)/shard_map/all_gather | solution.py:194
  64.5 13.4 %copy-start.17 = (bf16[512,768]{1,0:T(8,128)(2,1)}, bf16[512,768]{1,0:T(8,128)(2,1)S(1)}, u32[]{:S(2)}) copy-start(bf16[512,768]{1,0:T(8,128)(2,1)S(1)} %get-tuple-element.55) | copy-start | bytes 2359300
  81.0 57.8 %all-gather.9.cloned.1.call-start = ((), (), s32[]{:S(2)}) async-start(), calls=%async_computation.7 | async-start | bytes 3932160 | tf_op jit(solution)/shard_map/all_gather | solution.py:195
  84.1 111.6 %all-gather.13.cloned.1.call-start = ((), (), s32[]{:S(2)}) async-start(), calls=%async_computation.9 | async-start | bytes 1216512 | tf_op jit(solution)/shard_map/all_gather | solution.py:126
  84.7 176.4 %all-gather.15.cloned.1.call-start = ((), (), s32[]{:S(2)}) async-start(), calls=%async_computation.10 | async-start | bytes 4866048 | tf_op jit(solution)/shard_map/all_gather | solution.py:130
  85.2 241.1 %all-gather.17.cloned.1.call-start = ((), (), s32[]{:S(2)}) async-start(), calls=%async_computation.11 | async-start | bytes 4866048 | tf_op jit(solution)/shard_map/all_gather | solution.py:132
  85.8 348.1 %reduce-scatter.7.cloned.1.call-start = ((), (), s32[]{:S(2)}) async-start(), calls=%async_computation.12 | async-start | bytes 3932160 | tf_op jit(solution)/shard_map/reduce_scatter | solution.py:239
  143.4 11.8 %copy-start.9 = (pred[2,256,1024]{2,1,0:T(8,128)(4,1)S(1)}, pred[2,256,1024]{2,1,0:T(8,128)(4,1)}, u32[]{:S(2)}) copy-start(pred[2,256,1024]{2,1,0:T(8,128)(4,1)} %compare_and_fusion) | copy-start | bytes 1572868
  326.3 10.0 %copy-start.7 = (f32[512,768]{1,0:T(8,128)S(1)}, f32[512,768]{1,0:T(8,128)}, u32[]{:S(2)}) copy-start(f32[512,768]{1,0:T(8,128)} %copy-done.6) | copy-start | bytes 4718596
  326.3 10.0 %copy-start.20 = (bf16[768,3072]{1,0:T(8,128)(2,1)S(1)}, bf16[768,3072]{1,0:T(8,128)(2,1)}, u32[]{:S(2)}) copy-start(bf16[768,3072]{1,0:T(8,128)(2,1)} %all-gather.15.cloned.1.call-done) | copy-start | bytes 14155780
  382.7 77.6 %reduce-scatter.9.cloned.1.call-start = ((), (), s32[]{:S(2)}) async-start(), calls=%async_computation.13 | async-start | bytes 3932160 | tf_op jit(solution)/shard_map/reduce_scatter | solution.py:242
  402.4 163.4 %reduce-scatter.13.cloned.1.call-start = ((), (), s32[]{:S(2)}) async-start(), calls=%async_computation.15 | async-start | bytes 2433024 | tf_op jit(solution)/shard_map/reduce_scatter | solution.py:266
  406.0 301.6 %reduce-scatter.15.cloned.1.call-start = ((), (), s32[]{:S(2)}) async-start(), calls=%async_computation.16 | async-start | bytes 9732096 | tf_op jit(solution)/shard_map/reduce_scatter | solution.py:270
  415.0 433.7 %reduce-scatter.17.cloned.1.call-start = ((), (), s32[]{:S(2)}) async-start(), calls=%async_computation.17 | async-start | bytes 9732096 | tf_op jit(solution)/shard_map/reduce_scatter | solution.py:272
  423.5 550.4 %reduce-scatter.11.cloned.1.call-start = ((), (), s32[]{:S(2)}) async-start(), calls=%async_computation.14 | async-start | bytes 7299072 | tf_op jit(solution)/shard_map/reduce_scatter | solution.py:263
  433.8 28.0 %copy-start.18 = (bf16[512,768]{1,0:T(8,128)(2,1)S(1)}, bf16[512,768]{1,0:T(8,128)(2,1)}, u32[]{:S(2)}) copy-start(bf16[512,768]{1,0:T(8,128)(2,1)} %copy-done.17) | copy-start | bytes 2359300
  435.4 31.3 %copy-start.13 = (bf16[512,768]{0,1:T(8,128)(2,1)}, bf16[512,768]{0,1:T(8,128)(2,1)S(1)}, u32[]{:S(2)}) copy-start(bf16[512,768]{0,1:T(8,128)(2,1)S(1)} %copy.66) | copy-start | bytes 2359300
  468.4 7.0 copy-start.11
  468.4 7.1 copy-start.3
  468.4 7.1 copy-start.14
  468.4 7.1 copy-start.16
  468.4 7.1 copy-start.21
  (12 other events, 26.6 us)
Sparse Core Ops, SparseCore 0:
  10.9 62.8 all-gather.6
  81.1 27.4 all-gather.10
  110.2 28.5 all-gather.8
  141.5 54.1 all-gather.12
  198.5 62.5 all-gather.14
  263.8 62.4 all-gather.16
  382.8 36.7 reduce-scatter.6
  422.3 37.9 reduce-scatter.8
  466.2 99.5 reduce-scatter.12
  573.1 134.4 reduce-scatter.14
  714.1 134.5 reduce-scatter.16
  855.7 118.1 reduce-scatter.10
where the time goes:
time: 988 us; the launch traced here: 981 us
  waiting for transfers between devices  656 us (66%)
  matrix products  141 us (14%)
  blocking collectives  87.9 us (9%)
  local copies, waits for them, and re-layouts  52.1 us (5%)
  other arithmetic  28.3 us (3%)
  between operations  15.1 us (2%)
    reduce_scatter x1, waiting for transfers between devices, body(): lax.psum_scatter(grad_up, ('seq', 'rows'), scatter_dimension=0, tiled=True)  142 us
    reduce_scatter x1, waiting for transfers between devices, body(): lax.psum_scatter(grad_down, ('seq', 'rows'), scatter_dimension=0, tiled=T...  141 us
    reduce_scatter x1, waiting for transfers between devices, body(): lax.psum_scatter(grad_project, ('seq', 'rows'), scatter_dimension=0, tile...  125 us
    unnamed x2, blocking collectives  82.8 us
    all_gather x1, waiting for transfers between devices, body(): lax.all_gather(up_weight, ('seq', 'rows'), axis=0, tiled=True)  61 us
    all_gather x1, waiting for transfers between devices, body(): lax.all_gather(down_weight, ('seq', 'rows'), axis=0, tiled=True)  57 us
    reduce_scatter x1, waiting for transfers between devices, body(): lax.psum_scatter(grad_out, ('seq', 'rows'), scatter_dimension=0, tiled=True)  38.4 us
    all_gather x1, waiting for transfers between devices, body(): lax.all_gather(value_rows, 'seq', axis=1, tiled=True)  26.7 us
  transfers between devices with their start and end apart: 12, of which 11 were waited for; matrix products, arithmetic and copies ran while one was open for 16% of the time, Pallas kernels for 0%

commit v1 on v0

v1 whole, which is shorter than its diff:
```python
import jax
import jax.numpy as jnp
from jax import lax
from jax.experimental import pallas as pl
from jax.experimental.pallas import tpu as pltpu
from jax.sharding import PartitionSpec as P

HEAD_SIZE = 64
LANES = 128
EPSILON = 1e-06
FLOOR_SCORE = -1e30
HALF_ROOT = 0.7071067811865476
EVERY = ("seq", "rows")
BF16 = jnp.bfloat16
F32 = jnp.float32


def dot(left, right, left_dim, right_dim):
    return lax.dot_general(
        left, right, (((left_dim,), (right_dim,)), ((), ())), preferred_element_type=F32
    )


def split_heads(pair):
    lane = lax.broadcasted_iota(jnp.int32, pair.shape, 1)
    zero = jnp.zeros_like(pair)
    return jnp.concatenate(
        [jnp.where(lane < HEAD_SIZE, pair, zero), jnp.where(lane < HEAD_SIZE, zero, pair)], axis=0
    )


def join_heads(both, count):
    row = lax.broadcasted_iota(jnp.int32, (both.shape[0], count), 0)
    return jnp.where(row < HEAD_SIZE, both[:, :count], both[:, count:]).T


def set_bias(key_segment, query_segment, bias):
    keys, asked = key_segment[0], query_segment[0]
    bias[...] = jnp.where((keys == asked) & (keys > 0.0), 0.0, FLOOR_SCORE)


def attend_kernel(q_ref, k_ref, v_ref, ks_ref, qs_ref, mix_ref, full_ref, lse_ref, bias, held):
    count, blocks, size = q_ref.shape[1], k_ref.shape[0], k_ref.shape[2]

    @pl.when(pl.program_id(1) == 0)
    def _():
        set_bias(ks_ref, qs_ref, bias)

    asked = split_heads(q_ref[0])
    top = None
    for j in range(blocks):
        rows = pl.ds(j * size, size)
        part = bias[rows, :]
        scores = dot(k_ref[j, 0], asked, 1, 1) + jnp.concatenate([part, part], axis=1)
        held[rows, :] = scores
        high = jnp.max(scores, axis=0, keepdims=True)
        top = high if top is None else jnp.maximum(top, high)
    total, mixed = 0.0, 0.0
    for j in range(blocks):
        weights = jnp.exp(held[pl.ds(j * size, size), :] - top)
        total = total + jnp.sum(weights, axis=0, keepdims=True)
        mixed = mixed + dot(v_ref[j, 0].T, weights.astype(BF16), 1, 0)
    live = qs_ref[0] > 0.0
    live = jnp.concatenate([live, live], axis=1)
    result = join_heads(mixed * jnp.where(live, 1.0 / total, 0.0), count)
    mix_ref[0] = result.astype(BF16)
    full_ref[0] = result
    lse_ref[0, 0] = jnp.where(live, top + jnp.log(total), 0.0)


def attend_back_kernel(
    q_ref, k_ref, v_ref, dm_ref, full_ref, lse_ref, ks_ref, qs_ref,
    dq_ref, dk_ref, dv_ref, qsum_ref, vsum_ref, bias,
):
    count, blocks, size = q_ref.shape[1], k_ref.shape[0], k_ref.shape[2]

    @pl.when(pl.program_id(1) == 0)
    def _():
        set_bias(ks_ref, qs_ref, bias)

    d_mixed = dm_ref[0]
    asked, pulled = split_heads(q_ref[0]), split_heads(d_mixed)
    product = (d_mixed.astype(F32) * full_ref[0]).T
    delta = jnp.concatenate(
        [
            jnp.sum(product[:HEAD_SIZE], axis=0, keepdims=True),
            jnp.sum(product[HEAD_SIZE:], axis=0, keepdims=True),
        ],
        axis=1,
    )
    lse = lse_ref[0, 0]
    d_query, v_sum = 0.0, 0.0
    for j in range(blocks):
        keys = k_ref[j, 0]
        part = bias[pl.ds(j * size, size), :]
        scores = dot(keys, asked, 1, 1) + jnp.concatenate([part, part], axis=1)
        probs = jnp.exp(scores - lse)
        d_probs = dot(v_ref[j, 0], pulled, 1, 1)
        d_scores = (probs * (d_probs - delta)).astype(BF16)
        d_value = dot(probs.astype(BF16), pulled, 1, 0)
        dv_ref[j, 0] = d_value.astype(BF16)
        dk_ref[j, 0] = dot(d_scores, asked, 1, 0).astype(BF16)
        v_sum = v_sum + jnp.sum(d_value, axis=0, keepdims=True)
        d_query = d_query + dot(keys.T, d_scores, 1, 0)
    d_query = join_heads(d_query, count) * HEAD_SIZE**-0.5
    dq_ref[0] = d_query.astype(BF16)
    qsum_ref[0, 0] = jnp.sum(d_query, axis=0, keepdims=True)
    vsum_ref[0, 0] = v_sum


def attention_specs(queries, key_values):
    rows, count, width = queries.shape
    blocks, _, size, _ = key_values.shape
    pairs = width // LANES
    tile = pl.BlockSpec((1, count, LANES), lambda r, p: (r, 0, p))
    keys = pl.BlockSpec((blocks, 1, size, LANES), lambda r, p: (0, r, 0, p))
    values = pl.BlockSpec((blocks, 1, size, LANES), lambda r, p: (0, r, 0, pairs + p))
    norm = pl.BlockSpec((1, 1, 1, 2 * count), lambda r, p: (r, p, 0, 0))
    key_segment = pl.BlockSpec((1, blocks * size, 1), lambda r, p: (r, 0, 0))
    query_segment = pl.BlockSpec((1, 1, count), lambda r, p: (r, 0, 0))
    column = pl.BlockSpec((1, 1, 1, LANES), lambda r, p: (r, p, 0, 0))
    return (rows, count, width, blocks, size, pairs), (
        tile, keys, values, norm, key_segment, query_segment, column,
    )


def attend(queries, key_values, key_segment, query_segment):
    sizes, specs = attention_specs(queries, key_values)
    rows, count, width, blocks, size, pairs = sizes
    tile, keys, values, norm, ks, qs, _ = specs
    area = rows * count * blocks * size
    return pl.pallas_call(
        attend_kernel,
        grid=(rows, pairs),
        in_specs=[tile, keys, values, ks, qs],
        out_specs=[tile, tile, norm],
        out_shape=[
            jax.ShapeDtypeStruct(queries.shape, BF16),
            jax.ShapeDtypeStruct(queries.shape, F32),
            jax.ShapeDtypeStruct((rows, pairs, 1, 2 * count), F32),
        ],
        scratch_shapes=[
            pltpu.VMEM((blocks * size, count), F32),
            pltpu.VMEM((blocks * size, 2 * count), F32),
        ],
        compiler_params=pltpu.CompilerParams(vmem_limit_bytes=24 * 2**20),
        cost_estimate=pl.CostEstimate(
            flops=16 * area * width,
            bytes_accessed=8 * rows * blocks * size * width,
            transcendentals=area * 12,
        ),
        name="attend",
    )(queries, key_values, key_values, key_segment, query_segment)


def attend_back(queries, key_values, d_mixed, mixed_full, lse, key_segment, query_segment):
    sizes, specs = attention_specs(queries, key_values)
    rows, count, width, blocks, size, pairs = sizes
    tile, keys, values, norm, ks, qs, column = specs
    area = rows * count * blocks * size
    grads = jax.ShapeDtypeStruct((blocks, rows, size, width), BF16)
    sums = jax.ShapeDtypeStruct((rows, pairs, 1, LANES), F32)
    return pl.pallas_call(
        attend_back_kernel,
        grid=(rows, pairs),
        in_specs=[tile, keys, values, tile, tile, norm, ks, qs],
        out_specs=[tile, keys, keys, column, column],
        out_shape=[jax.ShapeDtypeStruct(queries.shape, BF16), grads, grads, sums, sums],
        scratch_shapes=[pltpu.VMEM((blocks * size, count), F32)],
        compiler_params=pltpu.CompilerParams(vmem_limit_bytes=24 * 2**20),
        cost_estimate=pl.CostEstimate(
            flops=32 * area * width,
            bytes_accessed=16 * rows * blocks * size * width,
            transcendentals=area * 12,
        ),
        name="attend_back",
    )(queries, key_values, key_values, d_mixed, mixed_full, lse, key_segment, query_segment)


class Links:
    def __init__(self, seq, rows):
        self.sizes = {"seq": seq, "rows": rows}
        self.names = {}
        order = []
        for axis in EVERY:
            mask = self.sizes[axis] // 2
            while mask:
                order.append((axis, mask))
                mask //= 2
        self.order = order
        place = {axis: lax.axis_index(axis) for axis in EVERY}
        self.value = {(a, m): (place[a] // m) % 2 for a, m in order}
        self.near = [b for b in order if b == ("seq", 1)]
        self.first = [b for b in order if b[0] == "seq" and b[1] > 1]
        self.second = [b for b in order if b == ("rows", 1)]
        self.others = [b for b in order if b[0] == "rows" and b[1] > 1]

    def swap(self, array, bit):
        axis, mask = bit
        return lax.ppermute(array, axis, [(i, i ^ mask) for i in range(self.sizes[axis])])

    def gather(self, shard, bits):
        held, have = shard, []
        for bit in bits:
            other = self.swap(held, bit)
            upper = self.value[bit] == 1
            low = jnp.where(upper, other, held)
            high = jnp.where(upper, held, other)
            have = sorted([*have, bit], key=self.order.index)
            held = jnp.stack([low, high], axis=have.index(bit))
        return held.reshape(-1, shard.shape[-1])

    def scatter(self, terms, bits):
        have = list(self.order)
        held = terms.reshape((2,) * len(have) + (terms.shape[0] >> len(have), terms.shape[-1]))
        for bit in bits:
            at = have.index(bit)
            have.pop(at)
            mine = self.value[bit]
            sent = lax.dynamic_index_in_dim(held, 1 - mine, at, keepdims=False)
            kept = lax.dynamic_index_in_dim(held, mine, at, keepdims=False)
            other = self.swap(sent.astype(BF16), bit)
            held = kept.astype(F32) + other.astype(F32)
            if have:
                held = held.astype(BF16)
        return held


def layer_norm(inputs, gain, shift):
    mean = jnp.mean(inputs, axis=-1, keepdims=True)
    centered = inputs - mean
    spread = jnp.mean(centered * centered, axis=-1, keepdims=True)
    return centered * lax.rsqrt(spread + EPSILON) * gain + shift


def gelu_exact(inputs):
    return 0.5 * inputs * (1.0 + lax.erf(inputs * HALF_ROOT))


def body(
    patches, segments, masked, mask_embedding, norm1_gain, norm1_bias, qkv_weight, query_bias,
    value_bias, out_weight, out_bias, norm2_gain, norm2_bias, up_weight, up_bias, down_weight,
    down_bias, cotangent, *, seq, rows,
):
    links = Links(seq, rows)
    row_count, patch_count, width = patches.shape
    tokens = row_count * patch_count
    n = qkv_weight.shape[0]
    devices = seq * rows
    hidden_width = up_weight.shape[1]
    groups = hidden_width // width
    scale = HEAD_SIZE**-0.5
    near, first, second, others = links.near, links.first, links.second, links.others

    seq_bits = [*first, *near]
    small = [
        mask_embedding, norm1_gain, norm1_bias, query_bias, value_bias, out_bias, norm2_gain,
        norm2_bias, down_bias,
    ]
    columns = jnp.concatenate([jnp.stack(small), up_bias.reshape(groups, n)], axis=0).T
    columns = jnp.pad(columns, ((0, 0), (0, LANES - columns.shape[1])))
    cut = 3 * width // 2
    left = links.gather(qkv_weight[:, :cut], [*others, *second, *first, *near])
    right = links.gather(
        jnp.concatenate([qkv_weight[:, cut:], columns], axis=1),
        [*others, *first, *second, *near],
    )
    flags = (segments + 16 * masked).astype(BF16)
    rows_all = patches.reshape(1, tokens, width)
    flags_all = flags.reshape(1, row_count, patch_count)
    for bit in seq_bits:
        rows_all = jnp.concatenate([rows_all, links.swap(rows_all, bit)], axis=0)
        flags_all = jnp.concatenate([flags_all, links.swap(flags_all, bit)], axis=0)
    packed = jnp.concatenate(
        [
            out_weight,
            up_weight.reshape(n, groups, width).transpose(1, 0, 2).reshape(groups * n, width),
            down_weight,
        ],
        axis=0,
    )
    rest = lax.all_gather(packed, EVERY, axis=0, tiled=False)
    rest = rest.reshape(devices, -1, width)
    w_out = rest[:, :n].reshape(width, width)
    w_up = (
        rest[:, n : n + groups * n]
        .reshape(devices, groups, n, width)
        .transpose(0, 2, 1, 3)
        .reshape(width, hidden_width)
    )
    w_down = rest[:, n + groups * n :].reshape(hidden_width, width)

    vectors = right[:, width + width // 2 :].astype(F32).T
    embed, gain_one, shift_one, bias_query, bias_value, bias_out, gain_two, shift_two, bias_down = (
        vectors[i] for i in range(9)
    )
    bias_up = vectors[9 : 9 + groups].reshape(groups, devices, n).transpose(1, 0, 2).reshape(-1)
    w_project = jnp.concatenate([left, right[:, : width + width // 2]], axis=1)

    blocks = seq
    flags_all = flags_all.reshape(blocks, row_count, patch_count).astype(jnp.int32)
    masked_all = (flags_all >= 16).reshape(-1, 1)
    segments_all = (flags_all % 16).astype(F32)
    embedded_all = jnp.where(
        masked_all, embed[None, :], rows_all.reshape(-1, width).astype(F32)
    )
    mean_one = jnp.mean(embedded_all, axis=-1, keepdims=True)
    centered_one = embedded_all - mean_one
    rate_one = lax.rsqrt(jnp.mean(centered_one * centered_one, axis=-1, keepdims=True) + EPSILON)
    hat_one = centered_one * rate_one
    normed_all = (hat_one * gain_one + shift_one).astype(BF16)
    embedded = embedded_all[:tokens]
    normed_one = normed_all[:tokens]
    queries = ((dot(normed_one, w_project[:, :width], 1, 0) + bias_query) * scale).astype(BF16)
    shift_values = jnp.concatenate([jnp.zeros_like(bias_value), bias_value])
    key_values = (dot(normed_all, w_project[:, width:], 1, 0) + shift_values).astype(BF16)
    queries = queries.reshape(row_count, patch_count, width)
    key_values = key_values.reshape(blocks, row_count, patch_count, 2 * width)
    key_segment = segments_all.transpose(1, 0, 2).reshape(row_count, -1, 1)
    query_segment = segments_all[0].reshape(row_count, 1, patch_count)
    mixed3, mixed_full, lse = attend(queries, key_values, key_segment, query_segment)
    mixed = mixed3.reshape(tokens, width)

    middle = embedded + dot(mixed, w_out, 1, 0) + bias_out
    normed_mid, pull_two = jax.vjp(layer_norm, middle, gain_two, shift_two)
    normed_two = normed_mid.astype(BF16)
    hidden = dot(normed_two, w_up, 1, 0) + bias_up
    activated_full, pull_act = jax.vjp(gelu_exact, hidden)
    activated = activated_full.astype(BF16)
    result = middle + dot(activated, w_down, 1, 0) + bias_down
    output = result.astype(BF16).reshape(row_count, patch_count, width)

    d_branch = cotangent.reshape(tokens, width)
    d_result = d_branch.astype(F32)
    grad_down = dot(activated, d_branch, 0, 0).astype(BF16)
    grad_down_bias = jnp.sum(d_result, axis=0)
    (d_hidden_full,) = pull_act(dot(d_branch, w_down, 1, 1))
    d_hidden = d_hidden_full.astype(BF16)
    grad_up = dot(normed_two, d_hidden, 0, 0).astype(BF16)
    grad_up_bias = jnp.sum(d_hidden.astype(F32), axis=0)
    down_sum = links.scatter(grad_down, [*near, *first, *second, *others[::-1]])
    up_sum = links.scatter(grad_up, [*near, *second, *first, *others[::-1]])
    d_norm_mid, grad_gain_two, grad_shift_two = pull_two(dot(d_hidden, w_up, 1, 1))
    d_middle = d_result + d_norm_mid
    d_attn = d_middle.astype(BF16)
    grad_out = dot(mixed, d_attn, 0, 0).astype(BF16)
    grad_out_bias = jnp.sum(d_attn.astype(F32), axis=0)
    d_mixed = dot(d_attn, w_out, 1, 1).astype(BF16).reshape(row_count, patch_count, width)

    d_query, d_key, d_value, query_sums, value_sums = attend_back(
        queries, key_values, d_mixed, mixed_full, lse, key_segment, query_segment
    )
    d_query = d_query.reshape(tokens, width)
    d_key = d_key.reshape(-1, width)
    d_value = d_value.reshape(-1, width)
    grad_key = dot(normed_all, d_key, 0, 0).astype(BF16)
    grad_value = dot(normed_all, d_value, 0, 0).astype(BF16)
    grad_query = dot(normed_one, d_query, 0, 0).astype(BF16)
    kv_sum = links.scatter(
        jnp.concatenate([grad_key, grad_value], axis=1), [*near, *second, *first, *others[::-1]]
    )
    grad_query_bias = jnp.sum(query_sums, axis=0).reshape(-1)
    grad_value_bias = jnp.sum(value_sums, axis=0).reshape(-1)

    d_norm = dot(d_key, w_project[:, width : 2 * width], 1, 1) + dot(
        d_value, w_project[:, 2 * width :], 1, 1
    )
    d_own = dot(d_query, w_project[:, :width], 1, 1)
    d_norm = d_norm.at[:tokens].add(d_own)
    grad_gain_one = jnp.sum(d_norm * hat_one, axis=0)
    grad_shift_one = jnp.sum(d_norm, axis=0)
    pulled = d_norm * gain_one
    d_embedded = rate_one * (
        pulled
        - jnp.mean(pulled, axis=-1, keepdims=True)
        - hat_one * jnp.mean(pulled * hat_one, axis=-1, keepdims=True)
    )
    grad_embed = jnp.sum(jnp.where(masked_all, d_embedded, 0.0), axis=0) + jnp.sum(
        jnp.where(masked_all[:tokens], d_middle, 0.0), axis=0
    )
    held = d_embedded.astype(BF16).reshape(blocks, tokens, width)
    for bit in seq_bits[::-1]:
        half = held.shape[0] // 2
        other = links.swap(held[half:], bit)
        held = held[:half].astype(F32) + other.astype(F32)
        if half > 1:
            held = held.astype(BF16)
    input_grad = jnp.where(masked_all[:tokens], 0.0, d_middle + held.reshape(tokens, width))
    input_grad = input_grad.reshape(row_count, patch_count, width)

    small_grads = jnp.stack(
        [
            grad_embed, grad_gain_one, grad_shift_one, grad_query_bias, grad_value_bias,
            grad_out_bias, grad_gain_two, grad_shift_two, grad_down_bias,
        ]
    )
    grad_up_bias = grad_up_bias.reshape(devices, groups, n).transpose(1, 0, 2).reshape(groups, -1)
    small_grads = jnp.concatenate([small_grads, grad_up_bias], axis=0)
    filler = jnp.zeros((LANES - small_grads.shape[0], width), F32)
    small_grads = jnp.concatenate([small_grads, filler], axis=0).T.astype(BF16)
    last_sum = links.scatter(
        jnp.concatenate([grad_query, grad_out, small_grads], axis=1),
        [*near, *first, *second, *others[::-1]],
    )
    project_sum = jnp.concatenate([last_sum[:, :width], kv_sum], axis=1)
    out_sum = last_sum[:, width : 2 * width]
    tail = last_sum[:, 2 * width :].T
    return (
        output, input_grad, tail[0], tail[1], tail[2], project_sum, tail[3], tail[4], out_sum,
        tail[5], tail[6], tail[7], up_sum, tail[9 : 9 + groups].reshape(-1), down_sum, tail[8],
    )


def solution(mesh):
    one, two = P(EVERY), P(EVERY, None)
    rows, flags = P("rows", "seq", None), P("rows", "seq")
    seq, row_groups = mesh.shape["seq"], mesh.shape["rows"]

    def run(*arguments):
        return body(*arguments, seq=seq, rows=row_groups)

    return jax.shard_map(
        run,
        mesh=mesh,
        in_specs=(
            rows, flags, flags, one, one, one, two, one, one, two, one, one, one, two, one, two,
            one, rows,
        ),
        out_specs=(
            rows, rows, one, one, one, two, one, one, two, one, one, one, two, one, two, one,
        ),
        check_vma=False,
    )
```

time: 988 us -> 358 us (0.36)
  waiting for transfers between devices: 656 us -> 104 us
  matrix products: 141 us -> 52.8 us
  blocking collectives: 87.9 us -> 0 us
  Pallas kernels: 0 us -> 38.9 us
  starting transfers between devices: 0.69 us -> 37.7 us
  other arithmetic: 28.3 us -> 48.5 us
    reduce_scatter x6 -> x0, waiting for transfers between devices: 472 us -> none  [the longest x1 142 us: body(): lax.psum_scatter(grad_up, ('seq', 'rows'), scatter_dimension=0, tiled=True)]
    all_gather x6 -> x1, waiting for transfers between devices: 182 us -> 1.18 us  [body(): rest = lax.all_gather(packed, EVERY, axis=0, tiled=False)]
    ppermute x0 -> x36, waiting for transfers between devices: none -> 103 us  [swap(): lax.ppermute(array, axis, [(i, i ^ mask) for i in range(self.sizes[axis])])]
    dot_general x18 -> x17, matrix products: 141 us -> 52.8 us  [dot(): lax.dot_general(left, right, (((left_dim,), (right_dim,)), ((), ())), pre...]
    unnamed x2 -> x0, blocking collectives: 82.8 us -> none
    pallas_call x0 -> x2, Pallas kernels: none -> 38.9 us  [the longest x1 22.6 us: attend_back(): pl.pallas_call(attend_back_kernel, grid=(rows, pairs), in_specs=[tile, ke...]
    ppermute x0 -> x36, starting transfers between devices: none -> 37.6 us  [swap(): lax.ppermute(array, axis, [(i, i ^ mask) for i in range(self.sizes[axis])])]
    convert_element_type x7 -> x0, local copies, waits for them, and re-layouts: 15.6 us -> none  [the longest x1 4.68 us: body(): value_grad.astype(jnp.bfloat16)]
  transfers between devices with their start and end apart: 12 -> 37, of which waited for: 11 -> 19; matrix products, arithmetic and copies ran while one was open for 16% -> 23% of each run, Pallas kernels for 0% -> 5%
where the time goes in v1:
time: 358 us; the launch traced here: 352 us
  waiting for transfers between devices  104 us (29%)
  local copies, waits for them, and re-layouts  54.4 us (15%)
  matrix products  52.8 us (15%)
  other arithmetic  48.5 us (14%)
  Pallas kernels  38.9 us (11%)
  starting transfers between devices  37.7 us (11%)
  between operations  15.7 us (4%)
    ppermute x36, waiting for transfers between devices, swap(): lax.ppermute(array, axis, [(i, i ^ mask) for i in range(self.sizes[axis])])  103 us
    dot_general x17, matrix products, dot(): lax.dot_general(left, right, (((left_dim,), (right_dim,)), ((), ())), pre...  52.8 us
    ppermute x36, starting transfers between devices, swap(): lax.ppermute(array, axis, [(i, i ^ mask) for i in range(self.sizes[axis])])  37.6 us
    pallas_call x1, Pallas kernels, attend_back(): pl.pallas_call(attend_back_kernel, grid=(rows, pairs), in_specs=[tile, ke...  22.6 us
    pallas_call x1, Pallas kernels, attend(): pl.pallas_call(attend_kernel, grid=(rows, pairs), in_specs=[tile, keys, v...  16.3 us
    unnamed x99, local copies, waits for them, and re-layouts  10.5 us
    convert_element_type x16, other arithmetic, scatter(): held = held.astype(BF16)  9.34 us
    convert_element_type x2, other arithmetic, body(): normed_all = (hat_one * gain_one + shift_one).astype(BF16)  8 us
  transfers between devices with their start and end apart: 37, of which 19 were waited for; matrix products, arithmetic and copies ran while one was open for 23% of the time, Pallas kernels for 5%

profile of v1, /device:TPU:0, one launch (start us, length us, event | category | flops | bytes accessed | tf_op | source)
XLA Modules:
  0.0 352.4 jit_solution(13250421229597847524)
XLA Ops:
  10.7 4.0 %collective-permute-start.9 = (bf16[24,1152]{1,0:T(8,128)(2,1)S(1)}, bf16[24,1152]{1,0:T(8,128)(2,1)S(1)}, u32[]{:S(2)}, u32[]{:S(2)}) collective-permute-start(bf16[24,1152]{1,0:T(8,128)(2,1)S(1)} %slice.160), channel_id=1, source_target_pairs={{0,4},{1,5},{2,6},{3,7},{4,0},{5,1},{6,2},{7,3},{8,12},{9,13},{10,... | collective-permute-start | bytes 165896 | tf_op jit(solution)/shard_map/ppermute | solution.py:200
  26.4 6.1 %collective-permute-done.2 = bf16[24,1280]{1,0:T(8,128)(2,1)S(1)} collective-permute-done((bf16[24,1280]{1,0:T(8,128)(2,1)S(1)}, bf16[24,1280]{1,0:T(8,128)(2,1)S(1)}, u32[]{:S(2)}, u32[]{:S(2)}) %collective-permute-start.2) | collective-permute-done | bytes 61472 | tf_op jit(solution)/shard_map/ppermute | solution.py:200
  42.3 8.5 %collective-permute-done.4 = bf16[2,2,24,1280]{3,2,1,0:T(8,128)(2,1)S(1)} collective-permute-done((bf16[2,2,24,1280]{3,2,1,0:T(8,128)(2,1)S(1)}, bf16[2,2,24,1280]{3,2,1,0:T(8,128)(2,1)S(1)}, u32[]{:S(2)}, u32[]{:S(2)}) %collective-permute-start.4) | collective-permute-done | bytes 245792 | tf_op jit(solution)/shard_map/ppermute | solution.py:200
  52.2 13.6 %collective-permute-done.12 = bf16[2,2,2,24,1152]{4,3,2,1,0:T(8,128)(2,1)S(1)} collective-permute-done((bf16[2,2,2,24,1152]{4,3,2,1,0:T(8,128)(2,1)S(1)}, bf16[2,2,2,24,1152]{4,3,2,1,0:T(8,128)(2,1)S(1)}, u32[]{:S(2)}, u32[]{:S(2)}) %collective-permute-start.12) | collective-permute-done | bytes 442400 | tf_op jit(solution)/shard_map/ppermute | solution.py:200
  78.1 4.9 %add_convert_fusion.2 = (bf16[2048,768]{1,0:T(8,128)(2,1)S(1)}, f32[2048,768]{1,0:T(8,128)}) fusion(f32[768]{0:T(1024)S(1)} %get-tuple-element.57, f32[768]{0:T(1024)S(1)} %get-tuple-element.58, f32[2048]{0:T(1024)S(1)} %bitcast.362, f32[2048]{0:T(1024)S(1)} %bitcast.365, f32[768]{0:T(1024)S(1)} %get-tuple-element.59, pred[2048]{0:T(1024)(128)(4,1)S(1)} %ge.20, ...), kind=kLoop, calls=%fused_computation.17 | loop fusion | flops 14155776 | bytes 12610560 | tf_op jit(solution)/shard_map/convert_element_type | solution.py:311
  86.9 5.5 %add_convert_fusion = bf16[2048,1536]{1,0:T(8,128)(2,1)S(1)} fusion(bf16[2048,768]{1,0:T(8,128)(2,1)S(1)} %get-tuple-element.81, f32[1536]{0:T(1024)S(1)} %concatenate.64, bf16[768,1152]{1,0:T(8,128)(2,1)S(1)} %bitcast.335, bf16[768,1152]{1,0:T(8,128)(2,1)S(1)} %copy-done.34), kind=kOutput, calls=%fused_computation | convolution fusion | flops 4842848256 | bytes 12982272 | tf_op jit(solution)/shard_map/dot_general | solution.py:19
  92.5 16.3 %attend.1 = (bf16[2,256,768]{2,1,0:T(8,128)(2,1)S(1)}, f32[2,256,768]{2,1,0:T(8,128)S(1)}, f32[2,6,1,512]{3,2,1,0:T(1,128)S(1)}) custom-call(bf16[2,256,768]{2,1,0:T(8,128)(2,1)S(1)} %bitcast.311, bf16[4,2,256,1536]{3,2,1,0:T(8,128)(2,1)S(1)} %bitcast.301, bf16[4,2,256,1536]{3,2,1,0:T(8,128)(2,1)S(1)} %bitcast.302, f32[2,1024,1]{2,1,0:T(8,128)S(1)} %reshape.647.ks_ref, ...), custom_call_target="tpu_custom_call" | custom-call | flops 6442450944 | bytes 12582912 | tf_op jit(solution)/shard_map/attend/pallas_call | solution.py:132
  115.1 6.6 %fusion.48 = (bf16[32,96,768]{2,1,0:T(8,128)(2,1)}, bf16[32,96,768]{2,1,0:T(8,128)(2,1)S(1)}) fusion(bf16[32,216,768]{2,1,0:T(8,128)(2,1)} %bitcast.325), kind=kLoop, calls=%fused_computation.217 | loop fusion | bytes 18874368 | tf_op jit(solution)/shard_map/slice | solution.py:291
  127.8 5.4 %multiply_convert_fusion = (bf16[512,3072]{1,0:T(8,128)(2,1)}, f32[512,3072]{1,0:T(8,128)S(1)}) fusion(f32[3072]{0:T(1024)S(1)} %add.361, bf16[768,3072]{1,0:T(8,128)(2,1)S(1)} %bitcast.339, f32[512,768]{1,0:T(8,128)S(1)} %get-tuple-element.115, f32[768]{0:T(1024)S(1)} %get-tuple-element.52, f32[768]{0:T(1024)S(1)} %get-tuple-element.53, ...), kind=kOutput, calls=%fused_computation.15 | convolution fusion | flops 2427322368 | bytes 15751168 | tf_op jit(solution)/shard_map/dot_general | solution.py:19
  133.2 5.3 %fusion.52 = (bf16[3072]{0:T(1024)(128)(2,1)S(1)}, bf16[512,3072]{1,0:T(8,128)(2,1)S(1)}) fusion(bf16[3072,768]{1,0:T(8,128)(2,1)S(1)} %bitcast.344, bf16[512,768]{1,0:T(8,128)(2,1)S(1)} %bitcast.350, f32[512,3072]{1,0:T(8,128)S(1)} %get-tuple-element.117, f32[3072]{0:T(1024)S(1)} %add.361), kind=kOutput, calls=%fused_computation.221 | convolution fusion | flops 2439508992 | bytes 14960640 | tf_op jit(solution)/shard_map/dot_general | solution.py:19
  141.6 4.9 %convolution_convert_fusion.1 = bf16[768,3072]{1,0:T(8,128)(2,1)} fusion(bf16[512,3072]{1,0:T(8,128)(2,1)S(1)} %get-tuple-element.120, f32[512,768]{1,0:T(8,128)S(1)} %get-tuple-element.115, f32[768]{0:T(1024)S(1)} %get-tuple-element.52, f32[768]{0:T(1024)S(1)} %get-tuple-element.53, f32[512]{0:T(512)S(1)} %fusion.39, f32[512]{0:T(512)S(1)} %broadcast_multiply_fusion.3), kind=kOutput, calls=%fused_computation.23 | convolution fusion | flops 2420244480 | bytes 9447424 | tf_op jit(solution)/shard_map/dot_general | solution.py:19
  150.4 22.6 %attend_back.1 = (bf16[2,256,768]{2,1,0:T(8,128)(2,1)S(1)}, bf16[4,2,256,768]{3,2,1,0:T(8,128)(2,1)S(1)}, bf16[4,2,256,768]{3,2,1,0:T(8,128)(2,1)S(1)}, f32[2,6,1,128]{3,2,1,0:T(1,128)S(1)}, f32[2,6,1,128]{3,2,1,0:T(1,128)S(1)}) custom-call(bf16[2,256,768]{2,1,0:T(8,128)(2,1)S(1)} %bitcast.312, bf16[4,2,256,1536]{3,2,1,0:T(8,128)(2,1)S(1)} %bitcast.305, ...), custom_call_target="tpu_custom_call" | custom-call | flops 12884901888 | bytes 25165824 | tf_op jit(solution)/shard_map/attend_back/pallas_call | solution.py:163
  185.7 5.6 %multiply_reduce_fusion = (bf16[768]{0:T(1024)(128)(2,1)S(1)}, f32[2048]{0:T(1024)S(1)}, f32[2048]{0:T(1024)S(1)}, bf16[768]{0:T(1024)(128)(2,1)S(1)}) fusion(f32[2048,768]{1,0:T(8,128)S(1)} %fusion.15, f32[2048]{0:T(1024)S(1)} %bitcast.363, f32[2048]{0:T(1024)S(1)} %bitcast.366, f32[768]{0:T(1024)S(1)} %get-tuple-element.59, pred[2048]{0:T(1024)(128)(4,1)S(1)} %ge.20, ...), kind=kLoop, calls=%fused_computation.11 | loop fusion | flops 25160192 | bytes 9481216 | tf_op jit(solution)/shard_map/reduce_sum | solution.py:370
  191.3 4.5 %select_reduce_fusion = (f32[768]{0:T(1024)S(1)}, bf16[2048,768]{1,0:T(8,128)(2,1)S(1)}) fusion(pred[2048]{0:T(1024)(128)(4,1)S(1)} %ge.20, f32[2048]{0:T(1024)S(1)} %get-tuple-element.121, f32[2048]{0:T(1024)S(1)} %bitcast.367, bf16[2,512,768]{2,1,0:T(8,128)(2,1)S(1)} %copy-done.4, bf16[1,512,768]{2,1,0:T(8,128)(2,1)S(1)} %copy-done.10, ...), kind=kLoop, calls=%fused_computation.12 | loop fusion | flops 22019328 | bytes 12626944 | tf_op jit(solution)/shard_map/reduce_sum | solution.py:378
  199.5 4.5 %copy.82 = bf16[768,1536]{1,0:T(8,128)(2,1)} copy(bf16[768,1536]{0,1:T(8,128)(2,1)} %pad_maximum_fusion.2) | data formatting | bytes 4718592 | tf_op jit(solution)/shard_map/concatenate | solution.py:360
  205.7 4.4 %constant_dynamic-slice_fusion.3 = (bf16[2,1,2,2,2,24,3072]{6,5,4,3,2,1,0:T(8,128)(2,1)}, bf16[2,1,2,2,2,24,3072]{6,5,4,3,2,1,0:T(8,128)(2,1)S(1)}) fusion(bf16[2,2,2,2,2,24,3072]{6,5,4,3,2,1,0:T(8,128)(2,1)} %bitcast.338, s32[]{:T(128)S(6)} %select_n.316, s32[]{:T(128)S(6)} %select_n.317), kind=kLoop, calls=%fused_computation.185 | loop fusion | bytes 9437192 | tf_op jit(solution)/shard_map/jit(dynamic_index_in_dim)/dynamic_slice | solution.py:221
  221.1 4.6 %convolution_convert_fusion = bf16[3072,768]{1,0:T(8,128)(2,1)S(1)} fusion(bf16[512,3072]{1,0:T(8,128)(2,1)} %get-tuple-element.116, bf16[512,768]{1,0:T(8,128)(2,1)S(1)} %bitcast.351), kind=kOutput, calls=%fused_computation.22 | convolution fusion | flops 2418278400 | bytes 8650752 | tf_op jit(solution)/shard_map/dot_general | solution.py:19
  225.7 7.3 %collective-permute-done.22 = bf16[2,2,2,24,1536]{4,3,2,1,0:T(8,128)(2,1)} collective-permute-done((bf16[2,2,2,24,1536]{4,3,2,1,0:T(8,128)(2,1)S(1)}, bf16[2,2,2,24,1536]{4,3,2,1,0:T(8,128)(2,1)}, u32[]{:S(2)}, u32[]{:S(2)}) %collective-permute-start.22) | collective-permute-done | bytes 589856 | tf_op jit(solution)/shard_map/ppermute | solution.py:200
  244.1 3.9 %collective-permute-done.24 = bf16[2,24,1536]{2,1,0:T(8,128)(2,1)S(1)} collective-permute-done((bf16[2,24,1536]{2,1,0:T(8,128)(2,1)S(1)}, bf16[2,24,1536]{2,1,0:T(8,128)(2,1)S(1)}, u32[]{:S(2)}, u32[]{:S(2)}) %collective-permute-start.24) | collective-permute-done | bytes 147488 | tf_op jit(solution)/shard_map/ppermute | solution.py:200
  261.4 11.0 %collective-permute-done.15 = bf16[1,512,768]{2,1,0:T(8,128)(2,1)S(1)} collective-permute-done((bf16[1,512,768]{2,1,0:T(8,128)(2,1)S(1)}, bf16[1,512,768]{2,1,0:T(8,128)(2,1)S(1)}, u32[]{:S(2)}, u32[]{:S(2)}) %collective-permute-start.15) | collective-permute-done | bytes 786464 | tf_op jit(solution)/shard_map/ppermute | solution.py:200
  284.8 13.0 %collective-permute-done.32 = bf16[2,2,2,96,768]{4,3,0,1,2:T(8,128)(2,1)} collective-permute-done((bf16[2,2,2,96,768]{4,3,0,1,2:T(8,128)(2,1)}, bf16[2,2,2,96,768]{4,3,0,1,2:T(8,128)(2,1)}, u32[]{:S(2)}, u32[]{:S(2)}) %collective-permute-start.32) | collective-permute-done | bytes 1179680 | tf_op jit(solution)/shard_map/ppermute | solution.py:200
  302.2 8.1 %collective-permute-done.28 = bf16[2,2,24,3072]{3,2,0,1:T(8,128)(2,1)S(1)} collective-permute-done((bf16[2,2,24,3072]{3,2,0,1:T(8,128)(2,1)S(1)}, bf16[2,2,24,3072]{3,2,0,1:T(8,128)(2,1)S(1)}, u32[]{:S(2)}, u32[]{:S(2)}) %collective-permute-start.28) | collective-permute-done | bytes 589856 | tf_op jit(solution)/shard_map/ppermute | solution.py:200
  312.9 7.2 %collective-permute-done.17 = bf16[2,2,2,24,1664]{4,3,2,1,0:T(8,128)(2,1)S(1)} collective-permute-done((bf16[2,2,2,24,1664]{4,3,2,1,0:T(8,128)(2,1)S(1)}, bf16[2,2,2,24,1664]{4,3,2,1,0:T(8,128)(2,1)S(1)}, u32[]{:S(2)}, u32[]{:S(2)}) %collective-permute-start.17) | collective-permute-done | bytes 639008 | tf_op jit(solution)/shard_map/ppermute | solution.py:200
  337.6 4.5 %collective-permute-done.20 = bf16[24,1664]{1,0:T(8,128)(2,1)S(1)} collective-permute-done((bf16[24,1664]{1,0:T(8,128)(2,1)S(1)}, bf16[24,1664]{1,0:T(8,128)(2,1)S(1)}, u32[]{:S(2)}, u32[]{:S(2)}) %collective-permute-start.20) | collective-permute-done | bytes 79904 | tf_op jit(solution)/shard_map/ppermute | solution.py:200
  (312 shorter events, 154.3 us)
Async XLA Ops:
  7.2 106.6 %all-gather.3.cloned.1.call-start = ((), (), s32[]{:S(2)}) async-start(), calls=%async_computation | async-start | bytes 10948608 | tf_op jit(solution)/shard_map/all_gather | solution.py:282
  10.7 13.6 %collective-permute-start.9 = (bf16[24,1152]{1,0:T(8,128)(2,1)S(1)}, bf16[24,1152]{1,0:T(8,128)(2,1)S(1)}, u32[]{:S(2)}, u32[]{:S(2)}) collective-permute-start(bf16[24,1152]{1,0:T(8,128)(2,1)S(1)} %slice.160), channel_id=1, source_target_pairs={{0,4},{1,5},{2,6},{3,7},{4,0},{5,1},{6,2},{7,3},{8,12},{9,13},{10,... | collective-permute-start | bytes 165896 | tf_op jit(solution)/shard_map/ppermute | solution.py:200
  17.0 49.8 %collective-permute-start.7 = (bf16[1,512,768]{2,1,0:T(8,128)(2,1)}, bf16[1,512,768]{2,1,0:T(8,128)(2,1)S(1)}, u32[]{:S(2)}, u32[]{:S(2)}) collective-permute-start(bf16[1,512,768]{2,1,0:T(8,128)(2,1)} %bitcast.314), channel_id=1, source_target_pairs={{0,16},{8,24},{16,0},{24,8},{1,17},{9,25},{17,1},{25,9},{2,18},{10... | collective-permute-start | bytes 2359304 | tf_op jit(solution)/shard_map/ppermute | solution.py:200
  24.4 9.1 %collective-permute-start.10 = (bf16[2,24,1152]{2,1,0:T(8,128)(2,1)S(1)}, bf16[2,24,1152]{2,1,0:T(8,128)(2,1)S(1)}, u32[]{:S(2)}, u32[]{:S(2)}) collective-permute-start(bf16[2,24,1152]{2,1,0:T(8,128)(2,1)S(1)} %pad_maximum_fusion.17), channel_id=1, source_target_pairs={{0,2},{1,3},{2,0},{3,1},{4,6},{5,7},{6,4},{7,5},{8,10},{9,11},{10,... | collective-permute-start | bytes 331784 | tf_op jit(solution)/shard_map/ppermute | solution.py:200
  39.3 11.4 %collective-permute-start.4 = (bf16[2,2,24,1280]{3,2,1,0:T(8,128)(2,1)S(1)}, bf16[2,2,24,1280]{3,2,1,0:T(8,128)(2,1)S(1)}, u32[]{:S(2)}, u32[]{:S(2)}) collective-permute-start(bf16[2,2,24,1280]{3,2,1,0:T(8,128)(2,1)S(1)} %pad_maximum_fusion.13), channel_id=1, source_target_pairs={{0,16},{8,24},{16,0},{24,8},{1,17},{9,25},{17,1},{25,9},{2,18},{10... | collective-permute-start | bytes 737288 | tf_op jit(solution)/shard_map/ppermute | solution.py:200
  41.1 24.7 %collective-permute-start.12 = (bf16[2,2,2,24,1152]{4,3,2,1,0:T(8,128)(2,1)S(1)}, bf16[2,2,2,24,1152]{4,3,2,1,0:T(8,128)(2,1)S(1)}, u32[]{:S(2)}, u32[]{:S(2)}) collective-permute-start(bf16[2,2,2,24,1152]{4,3,2,1,0:T(8,128)(2,1)S(1)} %pad_maximum_fusion.11), channel_id=1, source_target_pairs={{0,16},{8,24},{16,0},{24,8},{1,17},{9,25},{17,1},{25,9},{2,18},{10... | collective-permute-start | bytes 1327112 | tf_op jit(solution)/shard_map/ppermute | solution.py:200
  50.9 15.2 %collective-permute-start.5 = (bf16[2,2,2,24,1280]{4,3,2,1,0:T(8,128)(2,1)S(1)}, bf16[2,2,2,24,1280]{4,3,2,1,0:T(8,128)(2,1)S(1)}, u32[]{:S(2)}, u32[]{:S(2)}) collective-permute-start(bf16[2,2,2,24,1280]{4,3,2,1,0:T(8,128)(2,1)S(1)} %pad_maximum_fusion.10), channel_id=1, source_target_pairs={{0,1},{1,0},{2,3},{3,2},{4,5},{5,4},{6,7},{7,6},{8,9},{9,8},{10,11... | collective-permute-start | bytes 1474568 | tf_op jit(solution)/shard_map/ppermute | solution.py:200
  197.7 52.2 %collective-permute-start.14 = (bf16[2,512,768]{2,1,0:T(8,128)(2,1)}, bf16[2,512,768]{2,1,0:T(8,128)(2,1)}, u32[]{:S(2)}, u32[]{:S(2)}) collective-permute-start(bf16[2,512,768]{2,1,0:T(8,128)(2,1)} %bitcast.65), channel_id=1, source_target_pairs={{0,8},{8,0},{16,24},{24,16},{1,9},{9,1},{17,25},{25,17},{2,10},{10... | collective-permute-start | bytes 4718600 | tf_op jit(solution)/shard_map/ppermute | solution.py:200
  205.4 11.4 %collective-permute-start.21 = (bf16[2,2,2,2,24,1536]{5,4,3,2,1,0:T(8,128)(2,1)S(1)}, bf16[2,2,2,2,24,1536]{5,4,3,2,1,0:T(8,128)(2,1)S(1)}, u32[]{:S(2)}, u32[]{:S(2)}) collective-permute-start(bf16[2,2,2,2,24,1536]{5,4,3,2,1,0:T(8,128)(2,1)S(1)} %dynamic-slice_bitcast_fusion.3), channel_id=1, source_target_pairs={{0,8},{8,0},{16,24},{24,16},{1,9},{9,1},{17,25},{25,17},{2,10},{10... | collective-permute-start | bytes 3538952 | tf_op jit(solution)/shard_map/ppermute | solution.py:200
  211.7 41.6 %collective-permute-start.26 = (bf16[2,2,2,2,24,3072]{5,4,1,2,0,3:T(8,128)(2,1)}, bf16[2,2,2,2,24,3072]{5,4,1,2,0,3:T(8,128)(2,1)}, u32[]{:S(2)}, u32[]{:S(2)}) collective-permute-start(bf16[2,2,2,2,24,3072]{5,4,1,2,0,3:T(8,128)(2,1)} %bitcast.295), channel_id=1, source_target_pairs={{0,8},{8,0},{16,24},{24,16},{1,9},{9,1},{17,25},{25,17},{2,10},{10... | collective-permute-start | bytes 7077896 | tf_op jit(solution)/shard_map/ppermute | solution.py:200
  217.3 15.7 %collective-permute-start.22 = (bf16[2,2,2,24,1536]{4,3,2,1,0:T(8,128)(2,1)S(1)}, bf16[2,2,2,24,1536]{4,3,2,1,0:T(8,128)(2,1)}, u32[]{:S(2)}, u32[]{:S(2)}) collective-permute-start(bf16[2,2,2,24,1536]{4,3,2,1,0:T(8,128)(2,1)S(1)} %dynamic-slice_bitcast_fusion.7), channel_id=1, source_target_pairs={{0,1},{1,0},{2,3},{3,2},{4,5},{5,4},{6,7},{7,6},{8,9},{9,8},{10,11... | collective-permute-start | bytes 1769480 | tf_op jit(solution)/shard_map/ppermute | solution.py:200
  236.3 23.2 %collective-permute-start.31 = (bf16[2,2,2,2,96,768]{5,4,1,2,3,0:T(8,128)(2,1)S(1)}, bf16[2,2,2,2,96,768]{5,4,1,2,3,0:T(8,128)(2,1)S(1)}, u32[]{:S(2)}, u32[]{:S(2)}) collective-permute-start(bf16[2,2,2,2,96,768]{5,4,1,2,3,0:T(8,128)(2,1)S(1)} %bitcast.352), channel_id=1, source_target_pairs={{0,8},{8,0},{16,24},{24,16},{1,9},{9,1},{17,25},{25,17},{2,10},{10... | collective-permute-start | bytes 7077896 | tf_op jit(solution)/shard_map/ppermute | solution.py:200
  251.9 20.5 %collective-permute-start.15 = (bf16[1,512,768]{2,1,0:T(8,128)(2,1)S(1)}, bf16[1,512,768]{2,1,0:T(8,128)(2,1)S(1)}, u32[]{:S(2)}, u32[]{:S(2)}) collective-permute-start(bf16[1,512,768]{2,1,0:T(8,128)(2,1)S(1)} %slice.224), channel_id=1, source_target_pairs={{0,16},{8,24},{16,0},{24,8},{1,17},{9,25},{17,1},{25,9},{2,18},{10... | collective-permute-start | bytes 2359304 | tf_op jit(solution)/shard_map/ppermute | solution.py:200
  257.2 25.0 %collective-permute-start.27 = (bf16[2,2,2,24,3072]{4,3,1,2,0:T(8,128)(2,1)}, bf16[2,2,2,24,3072]{4,3,1,2,0:T(8,128)(2,1)}, u32[]{:S(2)}, u32[]{:S(2)}) collective-permute-start(bf16[2,2,2,24,3072]{4,3,1,2,0:T(8,128)(2,1)} %dynamic-slice_bitcast_fusion.2), channel_id=1, source_target_pairs={{0,1},{1,0},{2,3},{3,2},{4,5},{5,4},{6,7},{7,6},{8,9},{9,8},{10,11... | collective-permute-start | bytes 3538952 | tf_op jit(solution)/shard_map/ppermute | solution.py:200
  261.4 36.4 %collective-permute-start.32 = (bf16[2,2,2,96,768]{4,3,0,1,2:T(8,128)(2,1)}, bf16[2,2,2,96,768]{4,3,0,1,2:T(8,128)(2,1)}, u32[]{:S(2)}, u32[]{:S(2)}) collective-permute-start(bf16[2,2,2,96,768]{4,3,0,1,2:T(8,128)(2,1)} %dynamic-slice_bitcast_fusion.1), channel_id=1, source_target_pairs={{0,16},{8,24},{16,0},{24,8},{1,17},{9,25},{17,1},{25,9},{2,18},{10... | collective-permute-start | bytes 3538952 | tf_op jit(solution)/shard_map/ppermute | solution.py:200
  279.8 21.2 %collective-permute-start.16 = (bf16[2,2,2,2,24,1664]{5,4,3,2,1,0:T(8,128)(2,1)S(1)}, bf16[2,2,2,2,24,1664]{5,4,3,2,1,0:T(8,128)(2,1)S(1)}, u32[]{:S(2)}, u32[]{:S(2)}) collective-permute-start(bf16[2,2,2,2,24,1664]{5,4,3,2,1,0:T(8,128)(2,1)S(1)} %dynamic-slice_bitcast_fusion), channel_id=1, source_target_pairs={{0,8},{8,0},{16,24},{24,16},{1,9},{9,1},{17,25},{25,17},{2,10},{10... | collective-permute-start | bytes 3833864 | tf_op jit(solution)/shard_map/ppermute | solution.py:200
  283.9 26.4 %collective-permute-start.28 = (bf16[2,2,24,3072]{3,2,0,1:T(8,128)(2,1)S(1)}, bf16[2,2,24,3072]{3,2,0,1:T(8,128)(2,1)S(1)}, u32[]{:S(2)}, u32[]{:S(2)}) collective-permute-start(bf16[2,2,24,3072]{3,2,0,1:T(8,128)(2,1)S(1)} %dynamic-slice_bitcast_fusion.6), channel_id=1, source_target_pairs={{0,16},{8,24},{16,0},{24,8},{1,17},{9,25},{17,1},{25,9},{2,18},{10... | collective-permute-start | bytes 1769480 | tf_op jit(solution)/shard_map/ppermute | solution.py:200
  299.4 12.6 %collective-permute-start.33 = (bf16[2,2,96,768]{3,2,0,1:T(8,128)(2,1)S(1)}, bf16[2,2,96,768]{3,2,0,1:T(8,128)(2,1)S(1)}, u32[]{:S(2)}, u32[]{:S(2)}) collective-permute-start(bf16[2,2,96,768]{3,2,0,1:T(8,128)(2,1)S(1)} %dynamic-slice_bitcast_fusion.5), channel_id=1, source_target_pairs={{0,1},{1,0},{2,3},{3,2},{4,5},{5,4},{6,7},{7,6},{8,9},{9,8},{10,11... | collective-permute-start | bytes 1769480 | tf_op jit(solution)/shard_map/ppermute | solution.py:200
  301.4 18.7 %collective-permute-start.17 = (bf16[2,2,2,24,1664]{4,3,2,1,0:T(8,128)(2,1)S(1)}, bf16[2,2,2,24,1664]{4,3,2,1,0:T(8,128)(2,1)S(1)}, u32[]{:S(2)}, u32[]{:S(2)}) collective-permute-start(bf16[2,2,2,24,1664]{4,3,2,1,0:T(8,128)(2,1)S(1)} %dynamic-slice_bitcast_fusion.4), channel_id=1, source_target_pairs={{0,16},{8,24},{16,0},{24,8},{1,17},{9,25},{17,1},{25,9},{2,18},{10... | collective-permute-start | bytes 1916936 | tf_op jit(solution)/shard_map/ppermute | solution.py:200
  310.5 11.3 %collective-permute-start.29 = (bf16[2,24,3072]{2,1,0:T(8,128)(2,1)S(1)}, bf16[2,24,3072]{2,1,0:T(8,128)(2,1)S(1)}, u32[]{:S(2)}, u32[]{:S(2)}) collective-permute-start(bf16[2,24,3072]{2,1,0:T(8,128)(2,1)S(1)} %dynamic-slice_bitcast_fusion.10), channel_id=1, source_target_pairs={{0,2},{1,3},{2,0},{3,1},{4,6},{5,7},{6,4},{7,5},{8,10},{9,11},{10,... | collective-permute-start | bytes 884744 | tf_op jit(solution)/shard_map/ppermute | solution.py:200
  312.2 11.0 %collective-permute-start.34 = (bf16[2,96,768]{2,1,0:T(8,128)(2,1)S(1)}, bf16[2,96,768]{2,1,0:T(8,128)(2,1)S(1)}, u32[]{:S(2)}, u32[]{:S(2)}) collective-permute-start(bf16[2,96,768]{2,1,0:T(8,128)(2,1)S(1)} %dynamic-slice_bitcast_fusion.9), channel_id=1, source_target_pairs={{0,2},{1,3},{2,0},{3,1},{4,6},{5,7},{6,4},{7,5},{8,10},{9,11},{10,... | collective-permute-start | bytes 884744 | tf_op jit(solution)/shard_map/ppermute | solution.py:200
  322.0 10.7 %collective-permute-start.30 = (bf16[24,3072]{1,0:T(8,128)(2,1)S(1)}, bf16[24,3072]{1,0:T(8,128)(2,1)S(1)}, u32[]{:S(2)}, u32[]{:S(2)}) collective-permute-start(bf16[24,3072]{1,0:T(8,128)(2,1)S(1)} %dynamic-slice_bitcast_fusion.14), channel_id=1, source_target_pairs={{0,4},{1,5},{2,6},{3,7},{4,0},{5,1},{6,2},{7,3},{8,12},{9,13},{10,... | collective-permute-start | bytes 442376 | tf_op jit(solution)/shard_map/ppermute | solution.py:200
  323.3 13.5 %collective-permute-start.35 = (bf16[96,768]{1,0:T(8,128)(2,1)S(1)}, bf16[96,768]{1,0:T(8,128)(2,1)S(1)}, u32[]{:S(2)}, u32[]{:S(2)}) collective-permute-start(bf16[96,768]{1,0:T(8,128)(2,1)S(1)} %dynamic-slice_bitcast_fusion.13), channel_id=1, source_target_pairs={{0,4},{1,5},{2,6},{3,7},{4,0},{5,1},{6,2},{7,3},{8,12},{9,13},{10,... | collective-permute-start | bytes 442376 | tf_op jit(solution)/shard_map/ppermute | solution.py:200
  327.5 9.2 %collective-permute-start.19 = (bf16[2,24,1664]{2,1,0:T(8,128)(2,1)S(1)}, bf16[2,24,1664]{2,1,0:T(8,128)(2,1)S(1)}, u32[]{:S(2)}, u32[]{:S(2)}) collective-permute-start(bf16[2,24,1664]{2,1,0:T(8,128)(2,1)S(1)} %dynamic-slice_bitcast_fusion.12), channel_id=1, source_target_pairs={{0,2},{1,3},{2,0},{3,1},{4,6},{5,7},{6,4},{7,5},{8,10},{9,11},{10,... | collective-permute-start | bytes 479240 | tf_op jit(solution)/shard_map/ppermute | solution.py:200
  (60 other events, 393.2 us)
Sparse Core Ops, SparseCore 0:
  10.9 102.7 all-gather.2
